TPU v7x, 512 devices: a whole 4x8x8 slice. The times are simulated.
512 devices in a mesh: freq: 16 (over z, y_hi), strip: 32 (over x, y_lo, core).
Axes of the slice: x: 4, y: 8 (y_hi: 2, y_lo: 4; y = y_hi * 4 + y_lo), z: 8, core: 2. Of those that a mesh axis runs over, the one named last changes fastest.
Arguments:
- receiver_field: float32 [2, 16, 256, 2048], P(None, 'freq', 'strip'), may hold values from -17 to 17
- source_field: float32 [2, 16, 256, 2048], P(None, 'freq', 'strip'), may hold values from -4 to 4
- velocity_class: int32 [256, 2048], P('strip'), may hold values from 0 to 7
- filters: float32 [16, 8, 2, 9], P('freq'), may hold values from -0.8 to 0.8
- point_spread: float32 [16, 2, 15, 15], replicated, may hold values from -0.05 to 1
- spread_index: int32 [32, 16], replicated, may hold values from 0 to 15
Outputs:
- migrated: float32 [256, 2, 2048], P('strip', None, 'freq')
- reflectivity: float32 [256, 2, 2048], P('strip', None, 'freq')
- misfit: float32 [], replicated
All inputs are finite; a program needn't handle non-finite values.
Results may differ from a plain program's by a relative error of at most 0.0003.
Values sent between devices are 32-bit elements; how exact they have to be, the bound alone decides.
No kernel may reach another device: no remote copies, remote signals or barrier semaphores. Data moves between devices by JAX's collectives and lax.ppermute only.
A program may use at most 64 MiB of HBM per device.

v0:
```python
import math
import jax
import jax.numpy as jnp
from jax import lax
from jax.sharding import PartitionSpec as P

STEPS = 2
NCLASS = 8
PASSES = 2
HIGHEST = lax.Precision.HIGHEST


def extended_2(cells, sides, width):
    for axis, dim in sides:
        count = lax.axis_size(axis)
        ends = count - 1
        head = lax.slice_in_dim(cells, 0, width, axis=dim)
        tail = lax.slice_in_dim(cells, cells.shape[dim] - width, cells.shape[dim], axis=dim)
        cells = jnp.concatenate(
            [
                lax.ppermute(tail, axis, [(i, (i + 1) % count) for i in range(ends)]),
                cells,
                lax.ppermute(head, axis, [((i + 1) % count, i) for i in range(ends)]),
            ],
            axis=dim,
        )
    return cells


def class_maps(classes, filters):
    levels = jnp.arange(NCLASS, dtype=jnp.int32)
    chosen = jnp.where(classes[None] == levels[:, None, None], 1.0, 0.0)
    planes = jnp.einsum("fcpt,cxy->ptfxy", filters, chosen, precision=HIGHEST)
    taps_real = [planes[0, tap_index] for tap_index in range(9)]
    taps_imag = [planes[1, tap_index] for tap_index in range(9)]
    return (taps_real, taps_imag)


def advance(wavefield, taps_real, taps_imag, factor):
    row_count = wavefield.shape[2] - 2
    col_count = wavefield.shape[3]
    padded = jnp.pad(wavefield, ((0, 0), (0, 0), (0, 0), (1, 1)))
    real_part = jnp.zeros(taps_real[0].shape, jnp.float32)
    imag_part = jnp.zeros(taps_real[0].shape, jnp.float32)
    for tap_index in range(9):
        row_shift = tap_index // 3
        col_shift = tap_index % 3
        near_real = padded[
            0, :, row_shift : row_shift + row_count, col_shift : col_shift + col_count
        ]
        near_imag = padded[
            1, :, row_shift : row_shift + row_count, col_shift : col_shift + col_count
        ]
        coef_real = taps_real[tap_index]
        coef_imag = factor * taps_imag[tap_index]
        real_part = real_part + coef_real * near_real - coef_imag * near_imag
        imag_part = imag_part + coef_real * near_imag + coef_imag * near_real
    return jnp.stack([real_part, imag_part])


def correlate(receiver, source):
    return jnp.sum(receiver[0] * source[0] + receiver[1] * source[1], axis=0)


def lag_pick(lag_count):
    depths = jnp.arange(lag_count, dtype=jnp.int32)
    spacing = jnp.abs(depths[:, None] - depths[None, :])
    return jnp.where(spacing[None] == depths[:, None, None], 1.0, 0.0)


def convolve(extended, toeplitz, out_rows, picker):
    shifted = jnp.stack(
        [extended[shift_row : shift_row + out_rows] for shift_row in range(toeplitz.shape[0])],
        axis=2,
    )
    mixed = jnp.einsum("xdas,asly->xdly", shifted, toeplitz, precision=HIGHEST)
    return jnp.einsum("xdly,lde->xey", mixed, picker, precision=HIGHEST)


def local(receiver_field, source_field, velocity_class, filters, point_spread, spread_index):
    per_device = receiver_field.shape[1]
    row_count = receiver_field.shape[2]
    strips = lax.axis_size("strip")
    groups = lax.axis_size("freq")
    scaling = 1.0 / math.sqrt(per_device * groups)
    image_terms = []
    taps_real, taps_imag = class_maps(velocity_class, filters)
    receiver = receiver_field
    source = source_field
    for depth_step in range(STEPS):
        wide_receiver, wide_source = (
            extended_2(receiver, (("strip", 2),), 1),
            extended_2(source, (("strip", 2),), 1),
        )
        receiver = advance(wide_receiver, taps_real, taps_imag, 1.0)
        source = advance(wide_source, taps_real, taps_imag, -1.0)
        image_terms.append(correlate(receiver, source))
    partial_value = jnp.stack(image_terms, axis=1)
    whole = lax.psum(partial_value, "freq")
    share = whole.shape[2] // groups
    migrated = lax.dynamic_slice_in_dim(whole, lax.axis_index("freq") * share, share, 2)
    migrated = migrated * scaling
    col_count = migrated.shape[2]
    kernel_side = point_spread.shape[2]
    reach = kernel_side // 2
    wide_cols = col_count + 2 * reach
    picker = lag_pick(point_spread.shape[1])
    brick_row = lax.axis_index("strip")
    brick_col = lax.axis_index("freq")

    def brick_kernel(row_step, col_step):
        row_at = jnp.clip(brick_row + row_step, 0, strips - 1)
        col_at = jnp.clip(brick_col + col_step, 0, groups - 1)
        chosen = lax.dynamic_index_in_dim(
            lax.dynamic_index_in_dim(spread_index, row_at, 0, False), col_at, 0, False
        )
        return lax.dynamic_index_in_dim(point_spread, chosen, 0, False)

    columns = jnp.arange(wide_cols, dtype=jnp.int32)[:, None]
    outputs = jnp.arange(col_count, dtype=jnp.int32)[None, :]
    offsets = jnp.arange(kernel_side, dtype=jnp.int32)[:, None, None]
    band_forward = jnp.where(columns[None] - outputs[None] == offsets, 1.0, 0.0)
    band_adjoint = jnp.where(outputs[None] + 2 * reach - columns[None] == offsets, 1.0, 0.0)
    table_forward = jnp.einsum("lab,bsy->asly", brick_kernel(0, 0), band_forward, precision=HIGHEST)
    region = jnp.where(columns[:, 0] < reach, 0, jnp.where(columns[:, 0] < reach + col_count, 1, 2))
    region_pick = jnp.where(region[:, None] == jnp.arange(3, dtype=jnp.int32)[None, :], 1.0, 0.0)

    def table_adjoint(row_step):
        flipped = jnp.stack(
            [jnp.flip(brick_kernel(row_step, col_step), axis=1) for col_step in (-1, 0, 1)]
        )
        per_column = jnp.einsum("sj,jlab->slab", region_pick, flipped, precision=HIGHEST)
        return jnp.einsum("slab,bsw->aslw", per_column, band_adjoint, precision=HIGHEST)

    table_upper = table_adjoint(-1)
    table_middle = table_adjoint(0)
    table_lower = table_adjoint(1)

    def extend_rim(values):
        return extended_2(values, (("freq", 2), ("strip", 0)), reach)

    def measure(residual):
        return lax.psum(jnp.sum(residual * residual), ("freq", "strip"))

    cell_count = float(migrated.shape[1] * row_count * strips * col_count * groups)
    residual = -migrated
    reflectivity = jnp.zeros_like(migrated)
    energy = measure(residual)
    for pass_index in range(PASSES):
        weight = 1.0 / jnp.sqrt(residual * residual + energy / cell_count)
        extended = extend_rim(weight * residual)
        positions = jnp.arange(row_count + 2 * reach, dtype=jnp.int32)[:, None, None]
        middle = extended * jnp.where(
            (positions >= reach) & (positions < reach + row_count), 1.0, 0.0
        )
        summed = convolve(middle, table_middle, row_count, picker)
        upper = extended[: 3 * reach] * jnp.where(positions[: 3 * reach] < reach, 1.0, 0.0)
        lower = extended[row_count - reach :] * jnp.where(
            positions[row_count - reach :] >= row_count + reach, 1.0, 0.0
        )
        summed = summed.at[:reach].add(convolve(upper, table_upper, reach, picker))
        summed = summed.at[row_count - reach :].add(convolve(lower, table_lower, reach, picker))
        image_of = convolve(extend_rim(summed), table_forward, row_count, picker)
        grad_square, curvature = lax.psum(
            (jnp.sum(summed * summed), jnp.sum(weight * image_of * image_of)), ("freq", "strip")
        )
        step_length = grad_square / curvature
        reflectivity = reflectivity - step_length * summed
        residual = residual - step_length * image_of
        energy = measure(residual)
    return (migrated, reflectivity, energy / cell_count)


def solution(mesh):
    return jax.shard_map(
        local,
        mesh=mesh,
        in_specs=(
            P(None, "freq", "strip", None),
            P(None, "freq", "strip", None),
            P("strip", None),
            P("freq", None, None, None),
            P(),
            P(),
        ),
        out_specs=(P("strip", None, "freq"), P("strip", None, "freq"), P()),
        check_vma=False,
    )
```

profile of v0, /device:TPU:1, one launch (start us, length us, event | category | flops | bytes accessed | tf_op | source)
XLA Modules:
  0.0 950.9 jit_solution(10511014915909429593)
XLA Ops:
  8.9 4.6 collective-permute-start.2
  13.5 6.1 collective-permute-start.3
  23.1 3.0 collective-permute-start.1
  45.8 3.2 constant_dynamic-slice_fusion.2
  50.7 2.6 copy.115
  57.8 3.9 copy.109
  61.7 3.7 convolution_bitcast_fusion.2
  65.4 3.7 convolution_bitcast_fusion.3
  73.1 3.9 copy.102
  89.1 4.1 fusion.282
  93.2 2.6 collective-permute-start.6
  97.8 3.6 collective-permute-start.4
  103.8 2.7 collective-permute-done.5
  106.9 4.6 fusion.281
  112.3 5.4 convolution_bitcast_fusion.4
  117.8 193.8 %all-reduce.8.cloned.1.call-done = f32[8,2,2048]{2,1,0:T(2,128)} async-done(((f32[8,2,2048]{2,1,0:T(2,128)}), f32[8,2,2048]{2,1,0:T(2,128)}) %all-reduce.8.cloned.1.call-update) | async-done | bytes 131088 | tf_op jit(solution)/shard_map/psum | solution.py:99
  312.9 106.4 %psum.57 = f32[]{:T(128)} all-reduce(f32[]{:T(128)} %get-tuple-element.61), channel_id=1, replica_groups=mesh['freq'=16,'strip'=32] {'freq','strip'}, use_global_device_ids=true, to_apply=%region_2.3 | all-reduce | flops 1 | bytes 8 | tf_op jit(solution)/shard_map/psum | solution.py:143
  420.0 5.6 collective-permute-start.8
  427.0 7.0 collective-permute-done.9
  434.0 2.6 collective-permute-start.10
  436.7 2.8 collective-permute-start.11
  439.6 2.2 collective-permute-done.11
  442.5 4.2 fusion.14
  447.1 2.5 fusion.6
  449.5 2.5 fusion.10
  452.8 6.0 collective-permute-start.12
  462.1 5.0 collective-permute-done.13
  467.2 3.4 collective-permute-start.14
  470.5 2.1 collective-permute-start.15
  473.3 2.3 collective-permute-done.15
  476.0 2.4 fusion.2
  479.3 103.4 %all-reduce.5 = (f32[]{:T(128)}, f32[]{:T(128)}) all-reduce(f32[]{:T(128)} %multiply_reduce_fusion.2, f32[]{:T(128)} %get-tuple-element.117), channel_id=1, replica_groups=mesh['freq'=16,'strip'=32] {'freq','strip'}, use_global_device_ids=true, to_apply=%region_4.5 | all-reduce | flops 2 | bytes 16 | tf_op jit(solution)/shard_map/psum | solution.py:164
  584.6 95.3 %psum.60 = f32[]{:T(128)} all-reduce(f32[]{:T(128)} %get-tuple-element.57), channel_id=1, replica_groups=mesh['freq'=16,'strip'=32] {'freq','strip'}, use_global_device_ids=true, to_apply=%region_8.9 | all-reduce | flops 1 | bytes 8 | tf_op jit(solution)/shard_map/psum | solution.py:143
  680.6 4.8 collective-permute-start.16
  686.8 7.0 collective-permute-done.17
  693.9 2.6 collective-permute-start.18
  696.5 2.7 collective-permute-start.19
  699.2 2.3 collective-permute-done.19
  701.9 4.1 fusion.4
  706.3 2.5 fusion.8
  709.0 2.4 fusion.12
  712.4 6.5 collective-permute-start.20
  720.3 7.0 collective-permute-done.21
  727.4 3.4 collective-permute-start.22
  733.3 2.5 collective-permute-done.23
  736.2 2.4 fusion
  739.5 104.5 %all-reduce.4 = (f32[]{:T(128)}, f32[]{:T(128)}) all-reduce(f32[]{:T(128)} %multiply_reduce_fusion.1, f32[]{:T(128)} %get-tuple-element.119), channel_id=1, replica_groups=mesh['freq'=16,'strip'=32] {'freq','strip'}, use_global_device_ids=true, to_apply=%region_10.11 | all-reduce | flops 2 | bytes 16 | tf_op jit(solution)/shard_map/psum | solution.py:164
  846.6 95.3 %psum.63 = f32[]{:T(128)} all-reduce(f32[]{:T(128)} %multiply_reduce_fusion), channel_id=1, replica_groups=mesh['freq'=16,'strip'=32] {'freq','strip'}, use_global_device_ids=true, to_apply=%region_14.15 | all-reduce | flops 1 | bytes 8 | tf_op jit(solution)/shard_map/psum | solution.py:143
  (266 shorter events, 55.4 us)
Async XLA Ops:
  7.2 38.7 %copy-start.4 = (f32[16,2,15,15]{0,1,3,2:T(2,128)S(1)}, f32[16,2,15,15]{0,1,3,2:T(2,128)}, u32[]{:S(2)}) copy-start(f32[16,2,15,15]{0,1,3,2:T(2,128)} %param.18) | copy-start | bytes 86404
  7.2 304.4 %all-reduce.8.cloned.1.call-start = ((), (), s32[]{:S(2)}) async-start(), calls=%async_computation | async-start | bytes 262144 | tf_op jit(solution)/shard_map/psum | solution.py:99
  8.9 68.2 %collective-permute-start.2 = (f32[2,1,1,2048]{3,0,2,1:T(2,128)}, f32[2,1,1,2048]{3,0,2,1:T(2,128)}, u32[]{:S(2)}, u32[]{:S(2)}) collective-permute-start(f32[2,1,1,2048]{3,0,2,1:T(2,128)} %get-tuple-element.82), channel_id=1, source_target_pairs={{0,1},{1,2},{2,3},{3,4},{4,5},{5,6},{6,7},{7,8},{8,9},{9,10},{10,1... | collective-permute-start | bytes 49160 | tf_op jit(solution)/shard_map/ppermute | solution.py:21
  13.5 64.4 %collective-permute-start.3 = (f32[2,1,1,2048]{3,0,2,1:T(2,128)}, f32[2,1,1,2048]{3,0,2,1:T(2,128)}, u32[]{:S(2)}, u32[]{:S(2)}) collective-permute-start(f32[2,1,1,2048]{3,0,2,1:T(2,128)} %get-tuple-element.83), channel_id=1, source_target_pairs={{1,0},{2,1},{3,2},{4,3},{5,4},{6,5},{7,6},{8,7},{9,8},{10,9},{11,1... | collective-permute-start | bytes 49160 | tf_op jit(solution)/shard_map/ppermute | solution.py:23
  21.2 62.0 %collective-permute-start = (f32[2,1,1,2048]{3,0,2,1:T(2,128)}, f32[2,1,1,2048]{3,0,2,1:T(2,128)}, u32[]{:S(2)}, u32[]{:S(2)}) collective-permute-start(f32[2,1,1,2048]{3,0,2,1:T(2,128)} %get-tuple-element.78), channel_id=1, source_target_pairs={{0,1},{1,2},{2,3},{3,4},{4,5},{5,6},{6,7},{7,8},{8,9},{9,10},{10,1... | collective-permute-start | bytes 49160 | tf_op jit(solution)/shard_map/ppermute | solution.py:21
  23.1 61.0 %collective-permute-start.1 = (f32[2,1,1,2048]{3,0,2,1:T(2,128)}, f32[2,1,1,2048]{3,0,2,1:T(2,128)}, u32[]{:S(2)}, u32[]{:S(2)}) collective-permute-start(f32[2,1,1,2048]{3,0,2,1:T(2,128)} %get-tuple-element.79), channel_id=1, source_target_pairs={{1,0},{2,1},{3,2},{4,3},{5,4},{6,5},{7,6},{8,7},{9,8},{10,9},{11,1... | collective-permute-start | bytes 49160 | tf_op jit(solution)/shard_map/ppermute | solution.py:23
  49.1 4.3 copy-start.14
  61.7 3.7 copy-start.5
  65.4 3.8 copy-start.7
  65.4 4.1 copy-start.6
  65.4 5.8 copy-start.11
  65.4 5.8 copy-start.12
  71.2 6.6 copy-start.8
  79.6 4.3 copy-start.9
  93.2 10.1 %collective-permute-start.6 = (f32[2,1,1,2048]{3,0,2,1:T(2,128)S(1)}, f32[2,1,1,2048]{3,0,2,1:T(2,128)S(1)}, u32[]{:S(2)}, u32[]{:S(2)}) collective-permute-start(f32[2,1,1,2048]{3,0,2,1:T(2,128)S(1)} %get-tuple-element.73), channel_id=1, source_target_pairs={{0,1},{1,2},{2,3},{3,4},{4,5},{5,6},{6,7},{7,8},{8,9},{9,10},{10,1... | collective-permute-start | bytes 49160 | tf_op jit(solution)/shard_map/ppermute | solution.py:21
  95.8 7.6 collective-permute-start.7
  97.8 6.0 collective-permute-start.4
  101.4 5.1 collective-permute-start.5
  112.3 329.5 %copy-start.13 = (f32[21]{0:T(128)S(1)}, f32[21]{0:T(128)}, u32[]{:S(2)}) copy-start(f32[21]{0:T(128)} %fusion.337) | copy-start | bytes 256
  117.8 329.3 %copy-start.2 = (f32[15,142,2,128,1]{3,0,2,1,4:T(8,128)S(1)}, f32[15,142,2,128,1]{3,0,2,1,4:T(8,128)}, u32[]{:S(2)}) copy-start(f32[15,142,2,128,1]{3,0,2,1,4:T(8,128)} %convolution_bitcast_fusion.2) | copy-start | bytes 6543364
  312.9 271.1 %copy-start.10 = (f32[8,2,128]{2,1,0:T(2,128)}, f32[8,2,128]{2,1,0:T(2,128)S(1)}, u32[]{:S(2)}) copy-start(f32[8,2,128]{2,1,0:T(2,128)S(1)} %get-tuple-element.62) | copy-start | bytes 24580
  420.0 7.0 collective-permute-start.8
  425.6 8.3 collective-permute-start.9
  434.0 5.5 collective-permute-start.10
  436.7 5.0 collective-permute-start.11
  442.5 7.0 copy-start
  452.8 9.3 collective-permute-start.12
  458.7 8.3 collective-permute-start.13
  467.2 6.1 collective-permute-start.14
  470.5 5.0 collective-permute-start.15
  680.5 25.7 %copy-start.1 = (f32[15,142,2,128,1]{3,0,2,1,4:T(8,128)S(1)}, f32[15,142,2,128,1]{3,0,2,1,4:T(8,128)}, u32[]{:S(2)}) copy-start(f32[15,142,2,128,1]{3,0,2,1,4:T(8,128)} %convolution_bitcast_fusion.3) | copy-start | bytes 6543364
  680.6 6.1 collective-permute-start.16
  685.4 8.3 collective-permute-start.17
  693.9 5.3 collective-permute-start.18
  696.5 5.0 collective-permute-start.19
  706.1 2.9 copy-start.3
  712.4 7.8 collective-permute-start.20
  719.0 8.3 collective-permute-start.21
  727.4 5.9 collective-permute-start.22
  730.8 5.0 collective-permute-start.23
Sparse Core Ops, SparseCore 0:
  112.4 199.0 all-reduce.7
where the time goes:
time: 962 us; the launch traced here: 951 us
  blocking collectives  505 us (52%)
  waiting for transfers between devices  232 us (24%)
  starting transfers between devices  75.2 us (8%)
  matrix products  45.8 us (5%)
  between operations  38.4 us (4%)
  local copies, waits for them, and re-layouts  28.9 us (3%)
  other arithmetic  26 us (3%)
    psum x3, blocking collectives, measure(): return lax.psum(jnp.sum(residual * residual), ('freq', 'strip'))  297 us
    psum x2, blocking collectives, local(): lax.psum((jnp.sum(summed * summed), jnp.sum(weight * image_of * image_of)...  208 us
    psum x1, waiting for transfers between devices, local(): whole = lax.psum(partial_value, 'freq')  194 us
    ppermute x12, starting transfers between devices, extended_2(): lax.ppermute(tail, axis, [(i, (i + 1) % count) for i in range(ends)])  47.6 us
    ppermute x12, waiting for transfers between devices, extended_2(): lax.ppermute(head, axis, [((i + 1) % count, i) for i in range(ends)])  37.9 us
    ppermute x12, starting transfers between devices, extended_2(): lax.ppermute(head, axis, [((i + 1) % count, i) for i in range(ends)])  27.6 us
    dot_general x8, matrix products, convolve(): mixed = jnp.einsum('xdas,asly->xdly', shifted, toeplitz, precision=HIGHEST)  23 us
  transfers between devices with their start and end apart: 25, of which 10 were waited for; matrix products, arithmetic and copies ran while one was open for 5% of the time, Pallas kernels for 0%

commit v1 on v0

--- a/solution.py
+++ b/solution.py
@@ -96,7 +96,8 @@
         source = advance(wide_source, taps_real, taps_imag, -1.0)
         image_terms.append(correlate(receiver, source))
     partial_value = jnp.stack(image_terms, axis=1)
-    whole = lax.psum(partial_value, "freq")
+    parts = lax.all_gather(partial_value, "freq")
+    whole = jnp.sum(parts, axis=0)
     share = whole.shape[2] // groups
     migrated = lax.dynamic_slice_in_dim(whole, lax.axis_index("freq") * share, share, 2)
     migrated = migrated * scaling

time: 962 us -> 817 us (0.85)
  waiting for transfers between devices: 232 us -> 86.4 us
  matrix products: 45.8 us -> 56.4 us
    psum x1 -> x0, waiting for transfers between devices: 194 us -> none  [local(): whole = lax.psum(partial_value, 'freq')]
    all_gather x0 -> x1, waiting for transfers between devices: none -> 47.4 us  [local(): parts = lax.all_gather(partial_value, 'freq')]
    dot_general x3, matrix products: 12.9 us -> 24.7 us  [table_adjoint(): jnp.einsum('slab,bsw->aslw', per_column, band_adjoint, precision=HIGHEST)]
  transfers between devices with their start and end apart: 25 -> 25, of which waited for: 10 -> 10; matrix products, arithmetic and copies ran while one was open for 5% -> 7% of each run, Pallas kernels for 0% -> 0%
where the time goes in v1:
time: 817 us; the launch traced here: 808 us
  blocking collectives  499 us (61%)
  waiting for transfers between devices  86.4 us (11%)
  starting transfers between devices  75.5 us (9%)
  matrix products  56.4 us (7%)
  between operations  39.5 us (5%)
  other arithmetic  25.9 us (3%)
  local copies, waits for them, and re-layouts  25.2 us (3%)
    psum x3, blocking collectives, measure(): return lax.psum(jnp.sum(residual * residual), ('freq', 'strip'))  293 us
    psum x2, blocking collectives, local(): lax.psum((jnp.sum(summed * summed), jnp.sum(weight * image_of * image_of)...  206 us
    ppermute x12, starting transfers between devices, extended_2(): lax.ppermute(tail, axis, [(i, (i + 1) % count) for i in range(ends)])  49.9 us
    all_gather x1, waiting for transfers between devices, local(): parts = lax.all_gather(partial_value, 'freq')  47.4 us
    ppermute x12, waiting for transfers between devices, extended_2(): lax.ppermute(head, axis, [((i + 1) % count, i) for i in range(ends)])  39 us
    ppermute x12, starting transfers between devices, extended_2(): lax.ppermute(head, axis, [((i + 1) % count, i) for i in range(ends)])  25.6 us
    dot_general x3, matrix products, table_adjoint(): jnp.einsum('slab,bsw->aslw', per_column, band_adjoint, precision=HIGHEST)  24.7 us
    dot_general x8, matrix products, convolve(): mixed = jnp.einsum('xdas,asly->xdly', shifted, toeplitz, precision=HIGHEST)  22.6 us
  transfers between devices with their start and end apart: 25, of which 10 were waited for; matrix products, arithmetic and copies ran while one was open for 7% of the time, Pallas kernels for 0%

profile of v1, /device:TPU:1, one launch (start us, length us, event | category | flops | bytes accessed | tf_op | source)
XLA Modules:
  0.0 808.2 jit_solution(7308949430099930277)
XLA Ops:
  8.3 4.6 collective-permute-start.2
  12.9 5.5 collective-permute-start.3
  21.3 2.4 collective-permute-start.1
  23.7 2.7 convolution_bitcast_fusion
  34.3 4.1 fusion.295
  38.4 3.2 collective-permute-start.6
  43.6 3.6 collective-permute-start.4
  49.7 2.7 collective-permute-done.5
  52.8 4.9 fusion.294
  76.7 3.0 constant_dynamic-slice_fusion.2
  81.4 2.9 copy.506
  88.7 3.9 copy.495
  94.2 3.9 copy.484
  98.3 3.7 convolution_bitcast_fusion.2
  102.0 18.6 %convolution_bitcast_fusion.3 = f32[15,142,2,128]{3,0,2,1:T(8,128)} fusion(f32[142,2,15,15]{3,2,1,0:T(8,128)S(1)} %copy-done.5, s32[142,128]{1,0:T(8,128)S(1)} %iota_subtract_fusion.1), kind=kOutput, calls=%fused_computation.27 | convolution fusion | flops 98695680 | bytes 2509424 | tf_op jit(solution)/shard_map/slab,bsw->aslw/dot_general | solution.py:134
  120.6 2.3 convolution_bitcast_fusion.4
  123.0 47.4 %all-gather.3.cloned.1.call-done = f32[128,2,2048]{2,1,0:T(2,128)} async-done(((f32[8,2,2048]{2,1,0:T(2,128)}), f32[128,2,2048]{2,1,0:T(2,128)}) %all-gather.3.cloned.1.call-update) | async-done | bytes 2097168 | tf_op jit(solution)/shard_map/all_gather | solution.py:99
  170.3 2.6 reduce_sum.80
  173.6 101.9 %psum.49 = f32[]{:T(128)} all-reduce(f32[]{:T(128)} %multiply_reduce_fusion.3), channel_id=1, replica_groups=mesh['freq'=16,'strip'=32] {'freq','strip'}, use_global_device_ids=true, to_apply=%region_2.3 | all-reduce | flops 1 | bytes 8 | tf_op jit(solution)/shard_map/psum | solution.py:144
  276.2 3.7 collective-permute-start.8
  281.3 7.0 collective-permute-done.9
  288.4 4.6 collective-permute-start.10
  295.0 3.1 collective-permute-done.11
  298.6 4.1 fusion.44
  303.0 2.4 fusion.38
  306.0 2.4 fusion.32
  309.1 6.2 collective-permute-start.12
  318.6 5.0 collective-permute-done.13
  323.6 3.4 collective-permute-start.14
  329.5 2.5 collective-permute-done.15
  332.4 2.4 fusion.50
  335.7 102.6 %all-reduce.5 = (f32[]{:T(128)}, f32[]{:T(128)}) all-reduce(f32[]{:T(128)} %multiply_reduce_fusion.1, f32[]{:T(128)} %fusion.323), channel_id=1, replica_groups=mesh['freq'=16,'strip'=32] {'freq','strip'}, use_global_device_ids=true, to_apply=%region_4.5 | all-reduce | flops 2 | bytes 16 | tf_op jit(solution)/shard_map/psum | solution.py:165
  440.3 95.6 %psum.52 = f32[]{:T(128)} all-reduce(f32[]{:T(128)} %get-tuple-element.69), channel_id=1, replica_groups=mesh['freq'=16,'strip'=32] {'freq','strip'}, use_global_device_ids=true, to_apply=%region_8.9 | all-reduce | flops 1 | bytes 8 | tf_op jit(solution)/shard_map/psum | solution.py:144
  536.6 6.7 collective-permute-start.16
  544.7 7.0 collective-permute-done.17
  551.8 2.7 collective-permute-start.18
  554.4 2.8 collective-permute-start.19
  557.3 2.2 collective-permute-done.19
  559.9 4.1 fusion.47
  564.5 2.4 fusion.41
  567.4 2.4 fusion.35
  570.5 5.9 collective-permute-start.20
  577.7 7.0 collective-permute-done.21
  584.8 3.4 collective-permute-start.22
  590.7 2.5 collective-permute-done.23
  593.6 2.4 fusion.53
  597.5 103.8 %all-reduce.4 = (f32[]{:T(128)}, f32[]{:T(128)}) all-reduce(f32[]{:T(128)} %multiply_reduce_fusion, f32[]{:T(128)} %fusion.324), channel_id=1, replica_groups=mesh['freq'=16,'strip'=32] {'freq','strip'}, use_global_device_ids=true, to_apply=%region_10.11 | all-reduce | flops 2 | bytes 16 | tf_op jit(solution)/shard_map/psum | solution.py:165
  703.3 95.3 %psum.55 = f32[]{:T(128)} all-reduce(f32[]{:T(128)} %fusion.329), channel_id=1, replica_groups=mesh['freq'=16,'strip'=32] {'freq','strip'}, use_global_device_ids=true, to_apply=%region_14.15 | all-reduce | flops 1 | bytes 8 | tf_op jit(solution)/shard_map/psum | solution.py:144
  (278 shorter events, 49.1 us)
Async XLA Ops:
  7.2 19.3 %copy-start.7 = (f32[2,1,8,2048]{3,2,1,0:T(8,128)S(1)}, f32[2,1,8,2048]{3,2,1,0:T(8,128)}, u32[]{:S(2)}) copy-start(f32[2,1,8,2048]{3,2,1,0:T(8,128)} %param.15) | copy-start | bytes 393220
  7.2 163.1 %all-gather.3.cloned.1.call-start = ((), (), s32[]{:S(2)}) async-start(), calls=%async_computation | async-start | bytes 2228224 | tf_op jit(solution)/shard_map/all_gather | solution.py:99
  8.3 18.2 %collective-permute-start.2 = (f32[2,1,1,2048]{3,0,2,1:T(2,128)S(1)}, f32[2,1,1,2048]{3,0,2,1:T(2,128)S(1)}, u32[]{:S(2)}, u32[]{:S(2)}) collective-permute-start(f32[2,1,1,2048]{3,0,2,1:T(2,128)S(1)} %get-tuple-element.92), channel_id=1, source_target_pairs={{0,1},{1,2},{2,3},{3,4},{4,5},{5,6},{6,7},{7,8},{8,9},{9,10},{10,1... | collective-permute-start | bytes 49160 | tf_op jit(solution)/shard_map/ppermute | solution.py:21
  12.9 13.8 %collective-permute-start.3 = (f32[2,1,1,2048]{3,0,2,1:T(2,128)S(1)}, f32[2,1,1,2048]{3,0,2,1:T(2,128)S(1)}, u32[]{:S(2)}, u32[]{:S(2)}) collective-permute-start(f32[2,1,1,2048]{3,0,2,1:T(2,128)S(1)} %get-tuple-element.93), channel_id=1, source_target_pairs={{1,0},{2,1},{3,2},{4,3},{5,4},{6,5},{7,6},{8,7},{9,8},{10,9},{11,1... | collective-permute-start | bytes 49160 | tf_op jit(solution)/shard_map/ppermute | solution.py:23
  19.4 11.1 %collective-permute-start = (f32[2,1,1,2048]{3,0,2,1:T(2,128)S(1)}, f32[2,1,1,2048]{3,0,2,1:T(2,128)S(1)}, u32[]{:S(2)}, u32[]{:S(2)}) collective-permute-start(f32[2,1,1,2048]{3,0,2,1:T(2,128)S(1)} %get-tuple-element.88), channel_id=1, source_target_pairs={{0,1},{1,2},{2,3},{3,4},{4,5},{5,6},{6,7},{7,8},{8,9},{9,10},{10,1... | collective-permute-start | bytes 49160 | tf_op jit(solution)/shard_map/ppermute | solution.py:21
  21.3 9.4 %collective-permute-start.1 = (f32[2,1,1,2048]{3,0,2,1:T(2,128)S(1)}, f32[2,1,1,2048]{3,0,2,1:T(2,128)S(1)}, u32[]{:S(2)}, u32[]{:S(2)}) collective-permute-start(f32[2,1,1,2048]{3,0,2,1:T(2,128)S(1)} %get-tuple-element.89), channel_id=1, source_target_pairs={{1,0},{2,1},{3,2},{4,3},{5,4},{6,5},{7,6},{8,7},{9,8},{10,9},{11,1... | collective-permute-start | bytes 49160 | tf_op jit(solution)/shard_map/ppermute | solution.py:23
  26.9 3.6 copy-start.8
  38.4 10.9 %collective-permute-start.6 = (f32[2,1,1,2048]{3,0,2,1:T(2,128)S(1)}, f32[2,1,1,2048]{3,0,2,1:T(2,128)S(1)}, u32[]{:S(2)}, u32[]{:S(2)}) collective-permute-start(f32[2,1,1,2048]{3,0,2,1:T(2,128)S(1)} %get-tuple-element.83), channel_id=1, source_target_pairs={{0,1},{1,2},{2,3},{3,4},{4,5},{5,6},{6,7},{7,8},{8,9},{9,10},{10,1... | collective-permute-start | bytes 49160 | tf_op jit(solution)/shard_map/ppermute | solution.py:21
  41.6 7.7 collective-permute-start.7
  43.6 15.0 %copy-start.9 = (s32[32,16]{0,1:T(8,128)S(1)}, s32[32,16]{0,1:T(8,128)}, u32[]{:S(2)}) copy-start(s32[32,16]{0,1:T(8,128)} %param.19) | copy-start | bytes 6148
  43.6 6.1 collective-permute-start.4
  47.2 29.5 %copy-start.4 = (f32[16,2,15,15]{0,1,3,2:T(2,128)S(1)}, f32[16,2,15,15]{0,1,3,2:T(2,128)}, u32[]{:S(2)}) copy-start(f32[16,2,15,15]{0,1,3,2:T(2,128)} %param.18) | copy-start | bytes 86404
  47.2 5.2 collective-permute-start.5
  98.3 3.7 copy-start.5
  102.0 18.6 %copy-start.6 = (f32[142,2,15,15]{3,2,1,0:T(8,128)S(1)}, f32[142,2,15,15]{3,2,1,0:T(8,128)}, u32[]{:S(2)}) copy-start(f32[142,2,15,15]{3,2,1,0:T(8,128)} %copy.484) | copy-start | bytes 766804
  122.9 183.0 %copy-start = (f32[15,142,2,128]{3,0,2,1:T(8,128)}, f32[15,142,2,128]{3,0,2,1:T(8,128)S(1)}, u32[]{:S(2)}) copy-start(f32[15,142,2,128]{3,0,2,1:T(8,128)S(1)} %convolution_bitcast_fusion.4) | copy-start | bytes 6543364
  276.1 26.9 %copy-start.2 = (f32[15,142,2,128]{3,0,2,1:T(8,128)S(1)}, f32[15,142,2,128]{3,0,2,1:T(8,128)}, u32[]{:S(2)}) copy-start(f32[15,142,2,128]{3,0,2,1:T(8,128)} %convolution_bitcast_fusion.3) | copy-start | bytes 6543364
  276.2 5.0 collective-permute-start.8
  280.0 8.3 %collective-permute-start.9 = (f32[8,2,7]{2,0,1:T(8,128)S(1)}, f32[8,2,7]{2,0,1:T(8,128)S(1)}, u32[]{:S(2)}, u32[]{:S(2)}) collective-permute-start(f32[8,2,7]{2,0,1:T(8,128)S(1)} %get-tuple-element.131), channel_id=1, source_target_pairs={{32,0},{64,32},{96,64},{128,96},{160,128},{192,160},{224,192},{256... | collective-permute-start | bytes 1352 | tf_op jit(solution)/shard_map/ppermute | solution.py:23
  288.4 6.6 collective-permute-start.10
  293.0 5.1 collective-permute-start.11
  309.1 9.5 %collective-permute-start.12 = (f32[8,2,7]{2,0,1:T(8,128)S(1)}, f32[8,2,7]{2,0,1:T(8,128)S(1)}, u32[]{:S(2)}, u32[]{:S(2)}) collective-permute-start(f32[8,2,7]{2,0,1:T(8,128)S(1)} %get-tuple-element.117), channel_id=1, source_target_pairs={{0,32},{32,64},{64,96},{96,128},{128,160},{160,192},{192,224},{224... | collective-permute-start | bytes 1352 | tf_op jit(solution)/shard_map/ppermute | solution.py:21
  315.2 8.3 %collective-permute-start.13 = (f32[8,2,7]{2,0,1:T(8,128)S(1)}, f32[8,2,7]{2,0,1:T(8,128)S(1)}, u32[]{:S(2)}, u32[]{:S(2)}) collective-permute-start(f32[8,2,7]{2,0,1:T(8,128)S(1)} %get-tuple-element.118), channel_id=1, source_target_pairs={{32,0},{64,32},{96,64},{128,96},{160,128},{192,160},{224,192},{256... | collective-permute-start | bytes 1352 | tf_op jit(solution)/shard_map/ppermute | solution.py:23
  323.6 5.9 collective-permute-start.14
  327.0 5.1 collective-permute-start.15
  536.5 27.9 %copy-start.3 = (f32[15,142,2,128]{3,0,2,1:T(8,128)S(1)}, f32[15,142,2,128]{3,0,2,1:T(8,128)}, u32[]{:S(2)}) copy-start(f32[15,142,2,128]{3,0,2,1:T(8,128)} %convolution_bitcast_fusion.3) | copy-start | bytes 6543364
  536.6 8.0 collective-permute-start.16
  543.4 8.3 %collective-permute-start.17 = (f32[8,2,7]{2,0,1:T(8,128)S(1)}, f32[8,2,7]{2,0,1:T(8,128)S(1)}, u32[]{:S(2)}, u32[]{:S(2)}) collective-permute-start(f32[8,2,7]{2,0,1:T(8,128)S(1)} %get-tuple-element.115), channel_id=1, source_target_pairs={{32,0},{64,32},{96,64},{128,96},{160,128},{192,160},{224,192},{256... | collective-permute-start | bytes 1352 | tf_op jit(solution)/shard_map/ppermute | solution.py:23
  551.8 5.5 collective-permute-start.18
  554.4 5.1 collective-permute-start.19
  563.9 3.5 copy-start.1
  570.5 7.2 collective-permute-start.20
  576.4 8.3 %collective-permute-start.21 = (f32[8,2,7]{2,0,1:T(8,128)S(1)}, f32[8,2,7]{2,0,1:T(8,128)S(1)}, u32[]{:S(2)}, u32[]{:S(2)}) collective-permute-start(f32[8,2,7]{2,0,1:T(8,128)S(1)} %get-tuple-element.111), channel_id=1, source_target_pairs={{32,0},{64,32},{96,64},{128,96},{160,128},{192,160},{224,192},{256... | collective-permute-start | bytes 1352 | tf_op jit(solution)/shard_map/ppermute | solution.py:23
  584.8 5.9 collective-permute-start.22
  588.2 5.1 collective-permute-start.23
Sparse Core Ops, SparseCore 0:
  58.6 111.6 all-gather.2
